TPU v7x, 256 devices: a whole 4x4x8 slice. The times are simulated.
256 devices in a mesh: tm: 8 (over z), atom: 2 (over x_lo), chan: 16 (over y, x_hi, core).
Axes of the slice: x: 4 (x_hi: 2, x_lo: 2; x = x_hi * 2 + x_lo), y: 4, z: 8, core: 2. Of those that a mesh axis runs over, the one named last changes fastest.
Arguments:
- signal: bfloat16 [256, 8192], P('chan', 'tm'), may hold values from -6 to 6
- codes_init: float32 [128, 8192], P('atom', 'tm'), may hold values from -4 to 4
- atom_bank: bfloat16 [128, 256, 512], P('atom', 'chan'), may hold values from -0.015625 to 0.015625
- step_size: float32 [128], P('atom'), may hold values from 0.1 to 0.5
- threshold: float32 [128], P('atom'), may hold values from 0.3 to 3
Outputs:
- final_codes: float32 [128, 8192], P('atom', 'tm')
- residual: float32 [256, 8192], P('chan', 'tm')
All inputs are finite; a program needn't handle non-finite values.
Results may differ from a plain program's by a relative error of at most 0.0025.
Values may be sent and summed in bfloat16 or wider, within the bound.
A program may use at most 64 MiB of HBM per device.

v0:
```python
import jax
import jax.numpy as jnp
from jax import lax
from jax.sharding import PartitionSpec as P

ITERS = 2


def from_behind(value, axis, steps):
    count = lax.axis_size(axis)
    leading, last = (max(0, -steps), min(count, count - steps))
    return lax.ppermute(value, axis, [(source, source + steps) for source in range(leading, last)])


def synthesize(extended, atom_bank):
    atom_rows, chan_rows, taps = atom_bank.shape
    group = min(32, taps)
    turns = taps // group
    length = extended.shape[1] - taps + 1
    weights = (
        atom_bank.reshape(atom_rows, chan_rows, turns, group)
        .transpose(2, 1, 3, 0)
        .reshape(turns, chan_rows, group * atom_rows)
    )

    def synthesize_accumulate(turn_index, total):
        start = taps - group - turn_index * group
        window = lax.dynamic_slice_in_dim(extended, start, length + group - 1, 1)
        stacked = jnp.concatenate(
            [
                window[:, group - 1 - offset : group - 1 - offset + length]
                for offset in range(group)
            ],
            axis=0,
        )
        return total + jnp.dot(weights[turn_index], stacked, preferred_element_type=jnp.float32)

    return lax.fori_loop(
        0, turns, synthesize_accumulate, jnp.zeros((chan_rows, length), jnp.float32)
    )


def correlate(extended, atom_bank):
    atom_rows, chan_rows, taps = atom_bank.shape
    group = min(32, taps)
    turns = taps // group
    length = extended.shape[1] - taps + 1
    weights = (
        atom_bank.reshape(atom_rows, chan_rows, turns, group)
        .transpose(2, 0, 3, 1)
        .reshape(turns, atom_rows, group * chan_rows)
    )

    def correlate_accumulate(turn_index, total):
        start = turn_index * group
        window = lax.dynamic_slice_in_dim(extended, start, length + group - 1, 1)
        stacked = jnp.concatenate(
            [window[:, offset : offset + length] for offset in range(group)], axis=0
        )
        return total + jnp.dot(weights[turn_index], stacked, preferred_element_type=jnp.float32)

    return lax.fori_loop(
        0, turns, correlate_accumulate, jnp.zeros((atom_rows, length), jnp.float32)
    )


def shrink(current, gradient, step_size, threshold):
    moved = current - step_size[:, None] * gradient
    bound = (step_size * threshold)[:, None]
    return moved - jnp.clip(moved, -bound, bound)


def body(signal, codes_init, atom_bank, step_size, threshold):
    taps = atom_bank.shape[2]
    slab = signal.shape[1]
    current = codes_init
    misfit = None
    for sweep_index in range(ITERS):
        lowered = current.astype(jnp.bfloat16)
        earlier = from_behind(lowered[:, slab - taps + 1 :], "tm", 1)
        partial_recon = synthesize(jnp.concatenate([earlier, lowered], axis=1), atom_bank)
        recon = lax.psum(partial_recon, "atom")
        misfit = recon - signal.astype(jnp.float32)
        rounded = misfit.astype(jnp.bfloat16)
        following = from_behind(rounded[:, : taps - 1], "tm", -1)
        partial_grad = correlate(jnp.concatenate([rounded, following], axis=1), atom_bank)
        gradient = lax.psum(partial_grad, "chan")
        current = shrink(current, gradient, step_size, threshold)
    return (current, misfit)


def solution(mesh):
    placed = (P("chan", "tm"), P("atom", "tm"), P("atom", "chan", None), P("atom"), P("atom"))
    return jax.shard_map(
        body,
        mesh=mesh,
        in_specs=placed,
        out_specs=(P("atom", "tm"), P("chan", "tm")),
        check_vma=False,
    )
```

profile of v0, /device:TPU:1, one launch (start us, length us, event | category | flops | bytes accessed | tf_op | source)
XLA Modules:
  0.0 1402.1 jit_solution(5570843952976790271)
XLA Ops:
  8.3 4.4 collective-permute-start
  18.4 435.2 %while.60 = (s32[]{:T(128)}, f32[16,1024]{1,0:T(8,128)S(1)}, bf16[16,16,2048]{2,1,0:T(8,128)(2,1)}, bf16[64,1535]{1,0:T(8,128)(2,1)S(1)}, s32[]{:T(128)}, /*inde...) while((s32[]{:T(128)}, f32[16,1024]{1,0:T(8,128)S(1)}, ...), condition=%wide.region_1.0_spmd.clone, body=%wide.region_0.0_spmd.clone.sunk | while | flops 67141672 | bytes 12780941 | solution.py:38
  454.3 34.5 %all-reduce.5.cloned.1.call-done = f32[16,1024]{1,0:T(8,128)} async-done(((f32[16,1024]{1,0:T(8,128)}), f32[16,1024]{1,0:T(8,128)}) %all-reduce.5.cloned.1.call-update) | async-done | bytes 65552 | tf_op jit(solution)/shard_map/psum | solution.py:82
  495.4 61.8 %while.61 = (s32[]{:T(128)}, f32[64,1024]{1,0:T(8,128)S(1)}, bf16[16,64,512]{2,1,0:T(8,128)(2,1)}, bf16[16,1535]{1,0:T(8,128)(2,1)S(1)}, s32[]{:T(128)}, /*index...) while((s32[]{:T(128)}, f32[64,1024]{1,0:T(8,128)S(1)}, ...), condition=%wide.region_4.0_spmd.clone, body=%wide.region_3.0_spmd.clone.sunk | while | flops 67239976 | bytes 3736953 | solution.py:62
  558.0 145.2 %all-reduce.7.cloned.1.call-done = f32[64,1024]{1,0:T(8,128)} async-done(((f32[64,1024]{1,0:T(8,128)}), f32[64,1024]{1,0:T(8,128)}) %all-reduce.7.cloned.1.call-update) | async-done | bytes 262160 | tf_op jit(solution)/shard_map/psum | solution.py:87
  704.4 3.4 collective-permute-start.2
  709.0 435.2 %while.62 = (s32[]{:T(128)}, f32[16,1024]{1,0:T(8,128)S(1)}, bf16[16,16,2048]{2,1,0:T(8,128)(2,1)}, bf16[64,1535]{1,0:T(8,128)(2,1)S(1)}, s32[]{:T(128)}, /*inde...) while((s32[]{:T(128)}, f32[16,1024]{1,0:T(8,128)S(1)}, ...), condition=%wide.region_7.8_spmd.clone, body=%wide.region_6.7_spmd.clone.sunk | while | flops 67141672 | bytes 12780941 | solution.py:38
  733.4 2.9 convolution_add_fusion.10
  760.6 2.9 convolution_add_fusion.10
  787.8 2.9 convolution_add_fusion.10
  815.0 2.9 convolution_add_fusion.10
  842.2 2.9 convolution_add_fusion.10
  869.4 2.9 convolution_add_fusion.10
  896.6 2.9 convolution_add_fusion.10
  923.8 2.9 convolution_add_fusion.10
  951.0 2.9 convolution_add_fusion.10
  978.2 2.9 convolution_add_fusion.10
  1005.4 2.9 convolution_add_fusion.10
  1032.6 2.9 convolution_add_fusion.10
  1059.8 2.9 convolution_add_fusion.10
  1145.0 35.0 %all-reduce.9.cloned.1.call-done = f32[16,1024]{1,0:T(8,128)} async-done(((f32[16,1024]{1,0:T(8,128)}), f32[16,1024]{1,0:T(8,128)}) %all-reduce.9.cloned.1.call-update) | async-done | bytes 65552 | tf_op jit(solution)/shard_map/psum | solution.py:82
  1182.8 3.2 collective-permute-done.3
  1186.0 61.8 %while.63 = (s32[]{:T(128)}, f32[64,1024]{1,0:T(8,128)S(1)}, bf16[16,64,512]{2,1,0:T(8,128)(2,1)}, bf16[16,1535]{1,0:T(8,128)(2,1)S(1)}, s32[]{:T(128)}, /*index...) while((s32[]{:T(128)}, f32[64,1024]{1,0:T(8,128)S(1)}, ...), condition=%wide.region_10.11_spmd.clone, body=%wide.region_9.10_spmd.clone.sunk | while | flops 67239976 | bytes 3736953 | solution.py:62
  1248.5 145.2 %all-reduce.11.cloned.1.call-done = f32[64,1024]{1,0:T(8,128)} async-done(((f32[64,1024]{1,0:T(8,128)}), f32[64,1024]{1,0:T(8,128)}) %all-reduce.11.cloned.1.call-update) | async-done | bytes 262160 | tf_op jit(solution)/shard_map/psum | solution.py:87
  (2155 shorter events, 977.7 us)
Async XLA Ops:
  7.2 481.7 %all-reduce.5.cloned.1.call-start = ((), (), s32[]{:S(2)}) async-start(), calls=%async_computation | async-start | bytes 131072 | tf_op jit(solution)/shard_map/psum | solution.py:82
  8.3 10.0 collective-permute-start
  18.4 470.5 %copy-start.7 = (bf16[16,1024]{1,0:T(8,128)(2,1)S(1)}, bf16[16,1024]{1,0:T(8,128)(2,1)}, u32[]{:S(2)}) copy-start(bf16[16,1024]{1,0:T(8,128)(2,1)} %param.13) | copy-start | bytes 98308
  18.4 472.6 %copy-start.2 = (bf16[64,16,512]{2,1,0:T(8,128)(2,1)S(1)}, bf16[64,16,512]{2,1,0:T(8,128)(2,1)}, u32[]{:S(2)}) copy-start(bf16[64,16,512]{2,1,0:T(8,128)(2,1)} %param.15) | copy-start | bytes 3145732
  453.6 0.6 copy-start.3
  454.3 249.0 %all-reduce.7.cloned.1.call-start = ((), (), s32[]{:S(2)}) async-start(), calls=%async_computation.1 | async-start | bytes 524288 | tf_op jit(solution)/shard_map/psum | solution.py:87
  489.7 5.6 collective-permute-start.1
  495.3 62.7 %copy-start.8 = (f32[64]{0:T(128)S(1)}, f32[64]{0:T(128)}, u32[]{:S(2)}) copy-start(f32[64]{0:T(128)} %param.16) | copy-start | bytes 772
  495.3 62.7 %copy-start.9 = (f32[64]{0:T(128)S(1)}, f32[64]{0:T(128)}, u32[]{:S(2)}) copy-start(f32[64]{0:T(128)} %param.17) | copy-start | bytes 772
  495.3 207.9 %copy-start.5 = (f32[64,1024]{1,0:T(8,128)S(1)}, f32[64,1024]{1,0:T(8,128)}, u32[]{:S(2)}) copy-start(f32[64,1024]{1,0:T(8,128)} %param.14) | copy-start | bytes 786436
  557.2 0.7 copy-start
  557.9 622.0 %all-reduce.9.cloned.1.call-start = ((), (), s32[]{:S(2)}) async-start(), calls=%async_computation.2 | async-start | bytes 131072 | tf_op jit(solution)/shard_map/psum | solution.py:82
  704.4 4.5 collective-permute-start.2
  1144.2 0.6 copy-start.4
  1144.9 248.8 %all-reduce.11.cloned.1.call-start = ((), (), s32[]{:S(2)}) async-start(), calls=%async_computation.3 | async-start | bytes 524288 | tf_op jit(solution)/shard_map/psum | solution.py:87
  1181.5 4.5 collective-permute-start.3
  1185.9 207.8 %copy-start.6 = (f32[64,1024]{1,0:T(8,128)S(1)}, f32[64,1024]{1,0:T(8,128)}, u32[]{:S(2)}) copy-start(f32[64,1024]{1,0:T(8,128)} %all-reduce.7.cloned.1.call-done) | copy-start | bytes 786436
  1247.8 0.7 copy-start.1
Sparse Core Ops, SparseCore 0:
  454.4 34.3 all-reduce.4
  558.1 145.1 all-reduce.6
  1145.0 34.9 all-reduce.8
  1248.7 145.0 all-reduce.10
where the time goes:
time: 1400 us
  local copies, waits for them, and re-layouts  876 us (63%)
  waiting for transfers between devices  364 us (26%)
  matrix products  129 us (9%)
  between operations  14 us (1%)
    while x1984, local copies, waits for them, and re-layouts  836 us
    psum x2, waiting for transfers between devices, body(): gradient = lax.psum(partial_grad, 'chan')  290 us
    dot_general x32, matrix products, synthesize_accumulate(): jnp.dot(weights[turn_index], stacked, preferred_element_type=jnp.float32)  92.1 us
    psum x2, waiting for transfers between devices, body(): recon = lax.psum(partial_recon, 'atom')  69.5 us
    dot_general x32, matrix products, correlate_accumulate(): jnp.dot(weights[turn_index], stacked, preferred_element_type=jnp.float32)  37 us
  transfers between devices with their start and end apart: 8, of which 6 were waited for; matrix products, arithmetic and copies ran while one was open for 1% of the time, Pallas kernels for 0%

commit v1 on v0

--- a/solution.py
+++ b/solution.py
@@ -84,7 +84,8 @@
         rounded = misfit.astype(jnp.bfloat16)
         following = from_behind(rounded[:, : taps - 1], "tm", -1)
         partial_grad = correlate(jnp.concatenate([rounded, following], axis=1), atom_bank)
-        gradient = lax.psum(partial_grad, "chan")
+        terms = lax.all_gather(partial_grad, "chan", axis=0, tiled=False)
+        gradient = terms.sum(axis=0)
         current = shrink(current, gradient, step_size, threshold)
     return (current, misfit)
 

time: 1400 us -> 1240 us (0.89)
  waiting for transfers between devices: 364 us -> 198 us
    psum x2 -> x0, waiting for transfers between devices: 290 us -> none  [body(): gradient = lax.psum(partial_grad, 'chan')]
    all_gather x0 -> x2, waiting for transfers between devices: none -> 127 us  [body(): terms = lax.all_gather(partial_grad, 'chan', axis=0, tiled=False)]
where the time goes in v1:
time: 1240 us
  local copies, waits for them, and re-layouts  872 us (70%)
  waiting for transfers between devices  198 us (16%)
  matrix products  129 us (10%)
  between operations  14 us (1%)
    while x1984, local copies, waits for them, and re-layouts  832 us
    all_gather x2, waiting for transfers between devices, body(): terms = lax.all_gather(partial_grad, 'chan', axis=0, tiled=False)  127 us
    dot_general x32, matrix products, synthesize_accumulate(): jnp.dot(weights[turn_index], stacked, preferred_element_type=jnp.float32)  92.1 us
    psum x2, waiting for transfers between devices, body(): recon = lax.psum(partial_recon, 'atom')  67 us
    dot_general x32, matrix products, correlate_accumulate(): jnp.dot(weights[turn_index], stacked, preferred_element_type=jnp.float32)  37 us
  transfers between devices with their start and end apart: 8, of which 6 were waited for; matrix products, arithmetic and copies ran while one was open for 1% of the time, Pallas kernels for 0%

profile of v1, /device:TPU:1, one launch (start us, length us, event | category | flops | bytes accessed | tf_op | source)
XLA Modules:
  0.0 1235.2 jit_solution(4469470745625312910)
XLA Ops:
  8.3 4.4 collective-permute-start
  18.4 433.3 %while.60 = (s32[]{:T(128)}, f32[16,1024]{1,0:T(8,128)S(1)}, bf16[16,16,2048]{2,1,0:T(8,128)(2,1)}, bf16[64,1535]{1,0:T(8,128)(2,1)S(1)}, s32[]{:T(128)}, /*inde...) while((s32[]{:T(128)}, f32[16,1024]{1,0:T(8,128)S(1)}, ...), condition=%wide.region_1.0_spmd.clone, body=%wide.region_0.0_spmd.clone.sunk | while | flops 67141672 | bytes 12780941 | solution.py:38
  69.7 2.9 convolution_add_fusion.8
  96.8 2.9 convolution_add_fusion.8
  150.9 2.9 convolution_add_fusion.8
  178.0 2.9 convolution_add_fusion.8
  232.2 2.9 convolution_add_fusion.8
  286.3 2.9 convolution_add_fusion.8
  313.4 2.9 convolution_add_fusion.8
  367.5 2.9 convolution_add_fusion.8
  394.6 2.9 convolution_add_fusion.8
  448.8 2.9 convolution_add_fusion.8
  452.4 34.5 %all-reduce.3.cloned.1.call-done = f32[16,1024]{1,0:T(8,128)} async-done(((f32[16,1024]{1,0:T(8,128)}), f32[16,1024]{1,0:T(8,128)}) %all-reduce.3.cloned.1.call-update) | async-done | bytes 65552 | tf_op jit(solution)/shard_map/psum | solution.py:82
  493.4 61.8 %while.61 = (s32[]{:T(128)}, f32[64,1024]{1,0:T(8,128)S(1)}, bf16[16,64,512]{2,1,0:T(8,128)(2,1)}, bf16[16,1535]{1,0:T(8,128)(2,1)S(1)}, s32[]{:T(128)}, /*index...) while((s32[]{:T(128)}, f32[64,1024]{1,0:T(8,128)S(1)}, ...), condition=%wide.region_4.0_spmd.clone, body=%wide.region_3.0_spmd.clone.sunk | while | flops 67239976 | bytes 3736953 | solution.py:62
  556.1 63.4 %all-gather.5.cloned.1.call-done = f32[1024,1024]{1,0:T(8,128)} async-done(((f32[64,1024]{1,0:T(8,128)}), f32[1024,1024]{1,0:T(8,128)}) %all-gather.5.cloned.1.call-update) | async-done | bytes 4194320 | tf_op jit(solution)/shard_map/all_gather | solution.py:87
  622.2 3.4 collective-permute-start.2
  626.8 433.3 %while.62 = (s32[]{:T(128)}, f32[16,1024]{1,0:T(8,128)S(1)}, bf16[16,16,2048]{2,1,0:T(8,128)(2,1)}, bf16[64,1535]{1,0:T(8,128)(2,1)S(1)}, s32[]{:T(128)}, /*inde...) while((s32[]{:T(128)}, f32[16,1024]{1,0:T(8,128)S(1)}, ...), condition=%wide.region_7.8_spmd.clone, body=%wide.region_6.7_spmd.clone.sunk | while | flops 67141672 | bytes 12780941 | solution.py:38
  678.1 2.9 convolution_add_fusion.10
  705.2 2.9 convolution_add_fusion.10
  759.3 2.9 convolution_add_fusion.10
  1060.8 32.5 %all-reduce.5.cloned.1.call-done = f32[16,1024]{1,0:T(8,128)} async-done(((f32[16,1024]{1,0:T(8,128)}), f32[16,1024]{1,0:T(8,128)}) %all-reduce.5.cloned.1.call-update) | async-done | bytes 65552 | tf_op jit(solution)/shard_map/psum | solution.py:82
  1096.1 3.2 collective-permute-done.3
  1099.3 61.8 %while.63 = (s32[]{:T(128)}, f32[64,1024]{1,0:T(8,128)S(1)}, bf16[16,64,512]{2,1,0:T(8,128)(2,1)}, bf16[16,1535]{1,0:T(8,128)(2,1)S(1)}, s32[]{:T(128)}, /*index...) while((s32[]{:T(128)}, f32[64,1024]{1,0:T(8,128)S(1)}, ...), condition=%wide.region_10.11_spmd.clone, body=%wide.region_9.10_spmd.clone.sunk | while | flops 67239976 | bytes 3736953 | solution.py:62
  1161.9 63.5 %all-gather.7.cloned.1.call-done = f32[1024,1024]{1,0:T(8,128)} async-done(((f32[64,1024]{1,0:T(8,128)}), f32[1024,1024]{1,0:T(8,128)}) %all-gather.7.cloned.1.call-update) | async-done | bytes 4194320 | tf_op jit(solution)/shard_map/all_gather | solution.py:87
  (2155 shorter events, 976.9 us)
Async XLA Ops:
  7.2 479.7 %all-reduce.3.cloned.1.call-start = ((), (), s32[]{:S(2)}) async-start(), calls=%async_computation | async-start | bytes 131072 | tf_op jit(solution)/shard_map/psum | solution.py:82
  8.3 10.0 collective-permute-start
  18.4 468.5 %copy-start.6 = (bf16[16,1024]{1,0:T(8,128)(2,1)S(1)}, bf16[16,1024]{1,0:T(8,128)(2,1)}, u32[]{:S(2)}) copy-start(bf16[16,1024]{1,0:T(8,128)(2,1)} %param.13) | copy-start | bytes 98308
  18.4 470.7 %copy-start.2 = (bf16[64,16,512]{2,1,0:T(8,128)(2,1)S(1)}, bf16[64,16,512]{2,1,0:T(8,128)(2,1)}, u32[]{:S(2)}) copy-start(bf16[64,16,512]{2,1,0:T(8,128)(2,1)} %param.15) | copy-start | bytes 3145732
  451.7 0.6 copy-start.3
  452.3 167.2 %all-gather.5.cloned.1.call-start = ((), (), s32[]{:S(2)}) async-start(), calls=%async_computation.2 | async-start | bytes 4456448 | tf_op jit(solution)/shard_map/all_gather | solution.py:87
  487.7 5.6 collective-permute-start.1
  493.4 62.7 %copy-start.7 = (f32[64]{0:T(128)S(1)}, f32[64]{0:T(128)}, u32[]{:S(2)}) copy-start(f32[64]{0:T(128)} %param.16) | copy-start | bytes 772
  493.4 62.7 %copy-start.8 = (f32[64]{0:T(128)S(1)}, f32[64]{0:T(128)}, u32[]{:S(2)}) copy-start(f32[64]{0:T(128)} %param.17) | copy-start | bytes 772
  555.2 0.7 copy-start
  555.3 66.7 %copy-start.5 = (f32[64,1024]{1,0:T(8,128)S(1)}, f32[64,1024]{1,0:T(8,128)}, u32[]{:S(2)}) copy-start(f32[64,1024]{1,0:T(8,128)} %param.14) | copy-start | bytes 786436
  556.0 537.3 %all-reduce.5.cloned.1.call-start = ((), (), s32[]{:S(2)}) async-start(), calls=%async_computation.1 | async-start | bytes 131072 | tf_op jit(solution)/shard_map/psum | solution.py:82
  622.2 4.5 collective-permute-start.2
  1060.1 0.6 copy-start.4
  1060.8 164.6 %all-gather.7.cloned.1.call-start = ((), (), s32[]{:S(2)}) async-start(), calls=%async_computation.3 | async-start | bytes 4456448 | tf_op jit(solution)/shard_map/all_gather | solution.py:87
  1094.8 4.5 collective-permute-start.3
  1161.1 0.7 copy-start.1
Sparse Core Ops, SparseCore 0:
  452.4 34.3 all-reduce.2
  556.1 63.3 all-gather.4
  1060.9 32.4 all-reduce.4
  1162.0 63.2 all-gather.6
